TPU v7x, 32 devices: a whole 2x2x4 slice. The times are simulated.
32 devices in a mesh: rcv: 8 (over z, core), twin: 4 (over y, x).
Axes of the slice: x: 2, y: 2, z: 4, core: 2. Of those that a mesh axis runs over, the one named last changes fastest.
Arguments:
- record: bfloat16 [2048, 8, 2048], P('rcv', None, 'twin'), may hold values from -6 to 6
- slip_block: int32 [16], P('twin'), may hold values from 4 to 31, as said below
- ghost_lag: int32 [16, 4], P('twin'), may hold values from 1 to 35, as said below
- order_ops: bfloat16 [4, 512, 512], replicated, may hold values from -0.25 to 0.25
Outputs:
- denoised: bfloat16 [2048, 8, 2048], P('rcv', None, 'twin')
Inputs may be any that keep to these rules, and one draw needn't show every extreme that they name: `slip_block`: record r begins in a block b with b mod 4 = r // 4 and b // 4 >= 1; the 4 records of one twin index begin in distinct blocks. `ghost_lag`: among the records of one twin index, at most 5 pairs (r, h) with landing >= 0 land on blocks of one twin index; some twin index receives exactly 5 such pairs from every twin index.
All inputs are finite; a program needn't handle non-finite values.
Results may differ from a plain program's by a relative error of at most 0.009.
Values may be sent and summed in bfloat16 or wider, within the bound.
A program may use at most 128 MiB of HBM per device.

v0:
```python
import jax
import jax.numpy as jnp
from jax import lax
from jax.sharding import PartitionSpec as P


def with_halo(block, sides, width):
    for axis, dim in sides:
        count = lax.axis_size(axis)
        forward = [(i, i + 1) for i in range(count - 1)]
        backward = [(target, source) for source, target in forward]
        low = lax.ppermute(
            lax.slice_in_dim(block, block.shape[dim] - width, None, axis=dim), axis, forward
        )
        high = lax.ppermute(lax.slice_in_dim(block, 0, width, axis=dim), axis, backward)
        block = jnp.concatenate([low, block, high], axis=dim)
    return block


def landing_slots(slip_block, ghost_lag, twin_count):
    rec_count, order_count = ghost_lag.shape
    pair_total = rec_count * order_count
    slot_count = pair_total // twin_count + 1
    target = slip_block[:, None] - ghost_lag
    valid = target >= 0
    safe = jnp.maximum(target, 0)
    owner = jnp.where(valid, safe % twin_count, -1).reshape(pair_total)
    land_round = (safe // twin_count).reshape(pair_total)
    order_id = jnp.broadcast_to(
        jnp.arange(order_count, dtype=jnp.int32)[None, :], (rec_count, order_count)
    ).reshape(pair_total)
    position = jnp.arange(pair_total, dtype=jnp.int32)
    earlier = (owner[None, :] == owner[:, None]) & (position[None, :] < position[:, None])
    slot = jnp.sum(earlier.astype(jnp.int32), axis=1)
    chosen = (owner[:, None, None] == jnp.arange(twin_count, dtype=jnp.int32)[None, :, None]) & (
        slot[:, None, None] == jnp.arange(slot_count, dtype=jnp.int32)[None, None, :]
    )
    chosen_int = chosen.astype(jnp.int32)
    landed = jnp.sum(chosen_int * (land_round + 1)[:, None, None], axis=0) - 1
    orders = jnp.sum(chosen_int * (order_id + 1)[:, None, None], axis=0) - 1
    selector = chosen.astype(jnp.bfloat16).reshape(rec_count, order_count, twin_count, slot_count)
    return (selector, landed, orders)


def place_slots(arrived, arrived_rounds, rounds):
    hit = (arrived_rounds[:, :, None] == jnp.arange(rounds, dtype=jnp.int32)[None, None, :]).astype(
        jnp.bfloat16
    )
    return jnp.einsum("nsr,nscp->crp", hit, arrived, preferred_element_type=jnp.float32)


def local(record, slip_block, ghost_lag, order_ops):
    twin_count = lax.axis_size("twin")
    channels, rounds, samples = record.shape
    guides = jnp.moveaxis(jnp.take(record, slip_block // twin_count, axis=1), 1, 0)
    selector, landed, orders = landing_slots(slip_block, ghost_lag, twin_count)
    estimates = jnp.einsum(
        "jcp,hpq->jhcq", guides, order_ops, preferred_element_type=jnp.float32
    ).astype(jnp.bfloat16)
    outgoing = jnp.einsum(
        "jhns,jhcp->nscp", selector, estimates, preferred_element_type=jnp.float32
    ).astype(jnp.bfloat16)
    arrived, arrived_rounds = (
        lax.all_to_all(outgoing, "twin", split_axis=0, concat_axis=0, tiled=True),
        lax.all_to_all(landed, "twin", split_axis=0, concat_axis=0, tiled=True),
    )
    noise = place_slots(arrived, arrived_rounds, rounds)
    cleaned = (record.astype(jnp.float32) - noise).astype(jnp.bfloat16)
    padded = with_halo(cleaned, (("rcv", 0),), 1)
    widened = padded.astype(jnp.float32)
    smooth = 0.5 * widened[1:-1] + 0.25 * (widened[:-2] + widened[2:])
    return smooth.astype(jnp.bfloat16)


def solution(mesh):
    placed = (P("rcv", None, "twin"), P("twin"), P("twin", None), P())
    return jax.shard_map(
        local, mesh=mesh, in_specs=placed, out_specs=P("rcv", None, "twin"), check_vma=False
    )
```

profile of v0, /device:TPU:0, one launch (start us, length us, event | category | flops | bytes accessed | tf_op | source)
XLA Modules:
  0.0 110.1 jit_solution(3383143033374254660)
XLA Ops:
  0.0 0.0 copy-start
  0.0 0.9 fusion.20
  0.9 0.1 eq.87
  1.0 0.2 convert_reduce_fusion
  1.2 0.1 add.40
  1.3 0.2 select_reduce_fusion
  1.5 0.7 copy.14
  2.1 5.2 %all-to-all-start.1 = ((s32[4,1,5]{2,1,0:T(1,128)}), s32[4,1,5]{2,1,0:T(1,128)S(1)}, u32[]{:S(2)}, u32[]{:S(2)}) async-start(s32[4,1,5]{2,1,0:T(1,128)} %copy.14), calls=%async_computation.1 | async-start | bytes 4096 | tf_op jit(solution)/shard_map/all_to_all | solution.py:65
  7.3 0.7 compare_and_fusion
  8.0 0.1 eq.91
  8.1 0.1 iota_compare_fusion.1
  8.1 5.0 %gather_fusion = bf16[4,256,512]{2,0,1:T(4,128)(2,1)S(1)} fusion(bf16[256,8,512]{2,1,0:T(8,128)(2,1)} %param.4, s32[1024]{0:T(1024)S(1)} %pad_clamp_fusion), kind=kCustom, calls=%fused_computation | custom fusion | bytes 2097168 | tf_op jit(solution)/shard_map/jit(_take)/gather | solution.py:55
  13.1 0.5 select_bitcast_fusion
  13.6 0.0 copy-done
  13.7 2.3 %convert_bitcast_fusion = bf16[4,4,256,512,1]{3,2,1,0,4:T(8,128)(2,1)S(1)} fusion(bf16[4,512,512]{2,1,0:T(8,128)(2,1)S(1)} %copy-done, bf16[4,256,512,1]{2,0,1,3:T(4,128)(2,1)S(1)} %select_bitcast_fusion), kind=kOutput, calls=%fused_computation.12 | convolution fusion | flops 2149580800 | bytes 7340032 | tf_op jit(solution)/shard_map/jcp,hpq->jhcq/dot_general | solution.py:57
  16.0 9.0 %bitcast_convert_fusion = bf16[4,5,256,512]{3,1,0,2:T(8,128)(2,1)S(1)} fusion(bf16[4,4,256,512,1]{3,2,1,0,4:T(8,128)(2,1)S(1)} %convert_bitcast_fusion, pred[4,4,5]{2,1,0:T(4,128)(4,1)S(1)} %iota_compare_fusion.1, pred[4,4,4]{1,0,2:T(4,128)(4,1)S(1)} %iota_compare_fusion.3), kind=kOutput, calls=%fused_computation.1 | convolution fusion | flops 86507840 | bytes 9437328 | tf_op jit(solution)/shard_map/jhns,jhcp->nscp/dot_general | solution.py:60
  25.0 5.9 %copy.12 = bf16[4,5,256,512]{3,2,1,0:T(8,128)(2,1)} copy(bf16[4,5,256,512]{3,1,0,2:T(8,128)(2,1)S(1)} %bitcast_convert_fusion) | data formatting | bytes 10485760 | tf_op jit(solution)/shard_map/convert_element_type | solution.py:62
  30.8 0.0 all-to-all-done.1
  30.8 0.0 copy-start.1
  30.8 63.4 %all_to_all.11 = bf16[4,5,256,512]{3,2,1,0:T(8,128)(2,1)S(1)} all-to-all(bf16[4,5,256,512]{3,2,1,0:T(8,128)(2,1)} %copy.12), channel_id=1, replica_groups=mesh['rcv'=8,'twin'=4] {'twin'}, dimensions={0} | all-to-all | bytes 10485760 | tf_op jit(solution)/shard_map/all_to_all | solution.py:64
  94.3 0.0 copy-done.1
  94.3 7.3 %fusion.5 = bf16[256,8,512]{2,1,0:T(8,128)(2,1)S(1)} fusion(bf16[256,8,512]{2,1,0:T(8,128)(2,1)S(1)} %copy-done.1, bf16[4,5,256,512]{3,2,1,0:T(8,128)(2,1)S(1)} %all_to_all.11, s32[4,5]{1,0:T(4,128)S(1)} %bitcast.28), kind=kOutput, calls=%fused_computation.10 | convolution fusion | flops 45088928 | bytes 9437264 | tf_op jit(solution)/shard_map/nsr,nscp->crp/dot_general | solution.py:49
  101.6 1.3 %collective-permute-start = (bf16[1,8,512]{2,1,0:T(8,128)(2,1)S(1)}, bf16[1,8,512]{2,1,0:T(8,128)(2,1)S(1)}, u32[]{:S(2)}, u32[]{:S(2)}) collective-permute-start(bf16[1,8,512]{2,1,0:T(8,128)(2,1)S(1)} %get-tuple-element.7), channel_id=1, source_target_pairs={{0,4},{4,8},{8,12},{12,16},{16,20},{20,24},{24,28},{1,5},{5,9},{9,... | collective-permute-start | bytes 24584 | tf_op jit(solution)/shard_map/ppermute | solution.py:12
  102.9 1.3 %collective-permute-start.1 = (bf16[1,8,512]{2,1,0:T(8,128)(2,1)S(1)}, bf16[1,8,512]{2,1,0:T(8,128)(2,1)S(1)}, u32[]{:S(2)}, u32[]{:S(2)}) collective-permute-start(bf16[1,8,512]{2,1,0:T(8,128)(2,1)S(1)} %get-tuple-element.8), channel_id=1, source_target_pairs={{4,0},{8,4},{12,8},{16,12},{20,16},{24,20},{28,24},{5,1},{9,5},{13... | collective-permute-start | bytes 24584 | tf_op jit(solution)/shard_map/ppermute | solution.py:15
  104.2 0.0 collective-permute-done
  104.2 3.6 %collective-permute-done.1 = bf16[1,8,512]{2,1,0:T(8,128)(2,1)S(1)} collective-permute-done((bf16[1,8,512]{2,1,0:T(8,128)(2,1)S(1)}, bf16[1,8,512]{2,1,0:T(8,128)(2,1)S(1)}, u32[]{:S(2)}, u32[]{:S(2)}) %collective-permute-start.1) | collective-permute-done | bytes 8224 | tf_op jit(solution)/shard_map/ppermute | solution.py:15
  107.7 0.3 maximum_convert_fusion
  108.1 2.0 %fusion.4 = bf16[256,8,512]{2,1,0:T(8,128)(2,1)} fusion(f32[258,8,512]{2,1,0:T(8,128)S(1)} %maximum_convert_fusion), kind=kLoop, calls=%fused_computation.7 | loop fusion | flops 5242880 | bytes 14680064 | tf_op jit(solution)/shard_map/convert_element_type | solution.py:72
  (6 shorter events, 0.0 us)
Async XLA Ops:
  0.0 13.6 %copy-start = (bf16[4,512,512]{2,1,0:T(8,128)(2,1)S(1)}, bf16[4,512,512]{2,1,0:T(8,128)(2,1)}, u32[]{:S(2)}) copy-start(bf16[4,512,512]{2,1,0:T(8,128)(2,1)} %param.7) | copy-start | bytes 6291460
  2.1 28.7 %all-to-all-start.1 = ((s32[4,1,5]{2,1,0:T(1,128)}), s32[4,1,5]{2,1,0:T(1,128)S(1)}, u32[]{:S(2)}, u32[]{:S(2)}) async-start(s32[4,1,5]{2,1,0:T(1,128)} %copy.14), calls=%async_computation.1 | async-start | bytes 4096 | tf_op jit(solution)/shard_map/all_to_all | solution.py:65
  30.8 63.4 %copy-start.1 = (bf16[256,8,512]{2,1,0:T(8,128)(2,1)S(1)}, bf16[256,8,512]{2,1,0:T(8,128)(2,1)}, u32[]{:S(2)}) copy-start(bf16[256,8,512]{2,1,0:T(8,128)(2,1)} %param.4) | copy-start | bytes 6291460
  101.6 2.6 %collective-permute-start = (bf16[1,8,512]{2,1,0:T(8,128)(2,1)S(1)}, bf16[1,8,512]{2,1,0:T(8,128)(2,1)S(1)}, u32[]{:S(2)}, u32[]{:S(2)}) collective-permute-start(bf16[1,8,512]{2,1,0:T(8,128)(2,1)S(1)} %get-tuple-element.7), channel_id=1, source_target_pairs={{0,4},{4,8},{8,12},{12,16},{16,20},{20,24},{24,28},{1,5},{5,9},{9,... | collective-permute-start | bytes 24584 | tf_op jit(solution)/shard_map/ppermute | solution.py:12
  102.9 4.9 %collective-permute-start.1 = (bf16[1,8,512]{2,1,0:T(8,128)(2,1)S(1)}, bf16[1,8,512]{2,1,0:T(8,128)(2,1)S(1)}, u32[]{:S(2)}, u32[]{:S(2)}) collective-permute-start(bf16[1,8,512]{2,1,0:T(8,128)(2,1)S(1)} %get-tuple-element.8), channel_id=1, source_target_pairs={{4,0},{8,4},{12,8},{16,12},{20,16},{24,20},{28,24},{5,1},{9,5},{13... | collective-permute-start | bytes 24584 | tf_op jit(solution)/shard_map/ppermute | solution.py:15
where the time goes:
time: 112 us; the launch traced here: 110 us
  blocking collectives  63.4 us (57%)
  matrix products  18.6 us (17%)
  local copies, waits for them, and re-layouts  11.8 us (11%)
  starting transfers between devices  7.75 us (7%)
  other arithmetic  4.88 us (4%)
  waiting for transfers between devices  3.57 us (3%)
    all_to_all x1, blocking collectives, local(): lax.all_to_all(outgoing, 'twin', split_axis=0, concat_axis=0, tiled=True)  63.4 us
    dot_general x1, matrix products, local(): jnp.einsum('jhns,jhcp->nscp', selector, estimates, preferred_element_type...  8.95 us
    dot_general x1, matrix products, place_slots(): jnp.einsum('nsr,nscp->crp', hit, arrived, preferred_element_type=jnp.floa...  7.27 us
    convert_element_type x1, local copies, waits for them, and re-layouts, local(): outgoing = jnp.einsum('jhns,jhcp->nscp', selector, estimates, preferred_e...  5.87 us
    all_to_all x1, starting transfers between devices, local(): lax.all_to_all(landed, 'twin', split_axis=0, concat_axis=0, tiled=True)  5.16 us
    gather x1, local copies, waits for them, and re-layouts, local(): jnp.take(record, slip_block // twin_count, axis=1)  4.97 us
    ppermute x1, waiting for transfers between devices, with_halo(): lax.ppermute(lax.slice_in_dim(block, 0, width, axis=dim), axis, backward)  3.56 us
    dot_general x1, matrix products, local(): jnp.einsum('jcp,hpq->jhcq', guides, order_ops, preferred_element_type=jnp...  2.35 us
  transfers between devices with their start and end apart: 3, of which 1 were waited for; matrix products, arithmetic and copies ran while one was open for 21% of the time, Pallas kernels for 0%

commit v1 on v0

v1 whole, which is shorter than its diff:
```python
import functools

import jax
import jax.numpy as jnp
from jax import lax
from jax.experimental import pallas as pl
from jax.experimental.pallas import tpu as pltpu
from jax.sharding import PartitionSpec as P

MESH = pl.DeviceIdType.MESH
GROUP = 16
STEPS = 4
F32, BF16 = jnp.float32, jnp.bfloat16


def iota(shape, dim):
    return lax.broadcasted_iota(jnp.int32, shape, dim)


def clean_kernel(
    twins, lines, slip_ref, lag_ref, rec_ref, ops_hbm, out_ref,
    guides, lands, picks, spread, ops_ref, edges,
    ops_sem, land_send, land_recv, send_sem, recv_sem, edge_send, edge_recv,
):
    me = lax.axis_index("twin")
    line = lax.axis_index("rcv")
    recs, orders = lag_ref.shape
    rows, samples = rec_ref.shape
    groups, held, _ = guides.shape
    mine = held // twins
    rounds = rows // (groups * GROUP)
    block = GROUP * rounds
    per = groups // STEPS

    load_ops = pltpu.make_async_copy(ops_hbm, ops_ref, ops_sem)
    load_ops.start()

    others = [lax.rem(me + d, twins) for d in range(1, twins)]
    left, right = lax.rem(line + lines - 1, lines), lax.rem(line + 1, lines)
    barrier = pltpu.get_barrier_semaphore()
    for other in others:
        pl.semaphore_signal(barrier, inc=1, device_id={"twin": other}, device_id_type=MESH)
    for other in (left, right):
        pl.semaphore_signal(barrier, inc=1, device_id={"rcv": other}, device_id_type=MESH)

    order_row, rec_lane = iota((8, 128), 0), (iota((8, 128), 1) // GROUP) % recs
    land = jnp.full((8, 128), -1, jnp.int32)
    for r in range(recs):
        for h in range(orders):
            here = (order_row == h) & (rec_lane == r)
            land = jnp.where(here, slip_ref[r] - lag_ref[r, h], land)
    lands[me] = land

    row, col = iota((mine, block), 0), iota((mine, block), 1)
    slip = jnp.zeros((mine, block), jnp.int32)
    for r in range(recs):
        slip = jnp.where(row // GROUP == r, slip_ref[r], slip)
    pick = (row % GROUP == col // rounds) & ((col % rounds) * twins + me == slip)
    pick = jnp.where(pick, 1.0, 0.0).astype(BF16)

    def chunk(step):
        return lax.rem(step * (STEPS - 1), STEPS)

    def own(twin):
        return pl.ds(pl.multiple_of(twin * mine, mine), mine)

    def move(step, begin, count, twin, to, index):
        part = guides.at[pl.ds(chunk(step) * per + begin, count), own(twin)]
        return pltpu.make_async_remote_copy(
            src_ref=part, dst_ref=part, send_sem=send_sem.at[step, index],
            recv_sem=recv_sem.at[step, index], device_id={"twin": to}, device_id_type=MESH,
        )

    def extract(step):
        def one(i, _):
            g = chunk(step) * per + i
            rec = rec_ref[pl.ds(pl.multiple_of(g * block, block), block), :]
            guide = jnp.dot(pick, rec, preferred_element_type=F32)
            guides[g, own(me), :] = guide.astype(BF16)
            return 0
        lax.fori_loop(0, per, one, 0)

    relay = twins == 4
    if relay:
        across = (me // 2) * 2 + (1 - me % 2)
        along = (1 - me // 2) * 2 + me % 2
        half = per // 2

    def first_copies(step):
        if relay:
            return [move(step, 0, per, me, across, 0), move(step, 0, per, me, along, 1)]
        return [move(step, 0, per, me, other, d) for d, other in enumerate(others)]

    def relays(step):
        return [
            move(step, 0, half, along, across, 2),
            move(step, half, per - half, across, along, 3),
        ]

    extract(0)
    pl.semaphore_wait(barrier, twins + 1)
    for copy in first_copies(0):
        copy.start()

    def land_copy(d):
        return pltpu.make_async_remote_copy(
            src_ref=lands.at[me], dst_ref=lands.at[me], send_sem=land_send.at[d],
            recv_sem=land_recv.at[d], device_id={"twin": others[d]}, device_id_type=MESH,
        )

    for d in range(twins - 1):
        land_copy(d).start()

    def send_rest(step, _):
        extract(step)
        for copy in first_copies(step):
            copy.start()
        return 0

    lax.fori_loop(1, STEPS, send_rest, 0)

    for d in range(twins - 1):
        land_copy(d).wait()

    row, col = iota((block, 128), 0), iota((block, 128), 1)
    same = row // rounds == col % GROUP
    goal = (row % rounds) * twins + me
    per_tile = 128 // mine
    for tile in range(held // 128):
        for h in range(orders):
            got = lands[tile * per_tile, h : h + 1, :]
            got = jnp.broadcast_to(got, (block, 128))
            for k in range(1, per_tile):
                more = lands[tile * per_tile + k, h : h + 1, :]
                got = jnp.where(col // mine == k, jnp.broadcast_to(more, (block, 128)), got)
            hit = jnp.where(same & (got == goal), 1.0, 0.0).astype(BF16)
            picks[h * block : (h + 1) * block, tile * 128 : (tile + 1) * 128] = hit
    load_ops.wait()

    pad = 2 * rounds

    def work(step):
        def one(i, _):
            for k in range(2):
                g = chunk(step) * per + i * 2 + k
                landed = jnp.dot(picks[...], guides[g], preferred_element_type=F32).astype(BF16)
                for h in range(orders):
                    spread[k * block : (k + 1) * block, h * samples : (h + 1) * samples] = landed[
                        h * block : (h + 1) * block
                    ]
            noise = jnp.dot(spread[...], ops_ref[...], preferred_element_type=F32)
            at = (chunk(step) * per + i * 2) * block
            at = pl.multiple_of(at, 2 * block)
            rec = rec_ref[pl.ds(at, 2 * block), :].astype(F32)
            out_ref[pl.ds(pl.multiple_of(at + pad, pad), 2 * block), :] = (rec - noise).astype(BF16)
            return 0
        lax.fori_loop(0, per // 2, one, 0)

    def arrive(step):
        if relay:
            for copy in first_copies(step):
                copy.wait_recv()
            for copy in relays(step):
                copy.start()

    def finish(step):
        for copy in relays(step) if relay else first_copies(step):
            copy.wait_recv()

    def edge_copies():
        return [
            pltpu.make_async_remote_copy(
                src_ref=edges.at[k], dst_ref=edges.at[2 + k], send_sem=edge_send.at[k],
                recv_sem=edge_recv.at[k], device_id={"rcv": to}, device_id_type=MESH,
            )
            for k, to in enumerate((left, right))
        ]

    def advance(step, _):
        arrive(step + 1)
        finish(step)
        work(step)
        return 0

    arrive(0)
    lax.fori_loop(0, 2, advance, 0)
    edges[0] = out_ref[pad : 2 * pad, :]
    edges[1] = out_ref[rows : rows + pad, :]
    for copy in edge_copies():
        copy.start()
    lax.fori_loop(2, STEPS - 1, advance, 0)
    finish(STEPS - 1)
    work(STEPS - 1)

    for copy in edge_copies():
        copy.wait()
    zero = jnp.zeros((pad, samples), BF16)
    out_ref[0:pad, :] = jnp.where(line > 0, edges[3], zero)
    out_ref[rows + pad : rows + 2 * pad, :] = jnp.where(line < lines - 1, edges[2], zero)

    def sent(step, _):
        for copy in first_copies(step) + (relays(step) if relay else []):
            copy.wait_send()
        return 0

    lax.fori_loop(0, STEPS, sent, 0)


def local(record, slip_block, ghost_lag, order_ops):
    twins, lines = lax.axis_size("twin"), lax.axis_size("rcv")
    channels, rounds, samples = record.shape
    recs, orders = ghost_lag.shape
    groups, mine = channels // GROUP, recs * GROUP
    block = GROUP * rounds
    ways = max(twins, 4)
    vmem = pl.BlockSpec(memory_space=pltpu.VMEM)
    smem = pl.BlockSpec(memory_space=pltpu.SMEM)
    padded = pl.pallas_call(
        functools.partial(clean_kernel, twins, lines),
        out_shape=jax.ShapeDtypeStruct(((channels + 4) * rounds, samples), BF16),
        in_specs=[smem, smem, vmem, pl.BlockSpec(memory_space=pl.ANY)],
        out_specs=vmem,
        scratch_shapes=[
            pltpu.VMEM((groups, twins * mine, samples), BF16),
            pltpu.VMEM((twins, 8, 128), jnp.int32),
            pltpu.VMEM((orders * block, twins * mine), BF16),
            pltpu.VMEM((2 * block, orders * samples), BF16),
            pltpu.VMEM((orders * samples, samples), BF16),
            pltpu.VMEM((4, 2 * rounds, samples), BF16),
            pltpu.SemaphoreType.DMA,
            pltpu.SemaphoreType.DMA((twins,)),
            pltpu.SemaphoreType.DMA((twins,)),
            pltpu.SemaphoreType.DMA((STEPS, ways)),
            pltpu.SemaphoreType.DMA((STEPS, ways)),
            pltpu.SemaphoreType.DMA((2,)),
            pltpu.SemaphoreType.DMA((2,)),
        ],
        compiler_params=pltpu.CompilerParams(
            collective_id=0, has_side_effects=True, vmem_limit_bytes=48 * 2**20
        ),
        cost_estimate=pl.CostEstimate(
            flops=7 * 10**9, bytes_accessed=6 * 2**20, transcendentals=0
        ),
    )(
        slip_block, ghost_lag, record.reshape(channels * rounds, samples),
        order_ops.reshape(orders * samples, samples),
    )
    wide = padded.reshape(channels + 4, rounds, samples).astype(F32)
    middle = wide[2 : channels + 2]
    smooth = 0.5 * middle + 0.25 * (wide[1 : channels + 1] + wide[3 : channels + 3])
    return smooth.astype(BF16)


def solution(mesh):
    placed = (P("rcv", None, "twin"), P("twin"), P("twin", None), P())
    return jax.shard_map(
        local, mesh=mesh, in_specs=placed, out_specs=P("rcv", None, "twin"), check_vma=False
    )
```

time: 112 us -> 55 us (0.49); the launches traced: 110 us -> 54.8 us
  blocking collectives: 63.4 us -> 0 us
  Pallas kernels: 0 us -> 46.1 us
  matrix products: 18.6 us -> 0 us
  starting transfers between devices: 7.75 us -> 0 us
  local copies, waits for them, and re-layouts: 11.8 us -> 4.52 us
  waiting for transfers between devices: 3.57 us -> 0 us
    all_to_all x1 -> x0, blocking collectives: 63.4 us -> none  [local(): lax.all_to_all(outgoing, 'twin', split_axis=0, concat_axis=0, tiled=True)]
    pallas_call x0 -> x1, Pallas kernels: none -> 46.1 us  [local(): pl.pallas_call(functools.partial(clean_kernel, twins, lines), out_shape=j...]
    dot_general x3 -> x0, matrix products: 18.6 us -> none  [the longest x1 8.95 us: local(): jnp.einsum('jhns,jhcp->nscp', selector, estimates, preferred_element_type...]
    convert_element_type x1 -> x0, local copies, waits for them, and re-layouts: 5.87 us -> none  [local(): outgoing = jnp.einsum('jhns,jhcp->nscp', selector, estimates, preferred_e...]
    all_to_all x1 -> x0, starting transfers between devices: 5.16 us -> none  [local(): lax.all_to_all(landed, 'twin', split_axis=0, concat_axis=0, tiled=True)]
    gather x1 -> x0, local copies, waits for them, and re-layouts: 4.97 us -> none  [local(): jnp.take(record, slip_block // twin_count, axis=1)]
    unnamed x4 -> x8, local copies, waits for them, and re-layouts: 0.01 us -> 4.52 us
    ppermute x2 -> x0, waiting for transfers between devices: 3.56 us -> none  [the longest x1 3.56 us: with_halo(): lax.ppermute(lax.slice_in_dim(block, 0, width, axis=dim), axis, backward)]
  transfers between devices with their start and end apart: 3 -> 0, of which waited for: 1 -> 0; matrix products, arithmetic and copies ran while one was open for 21% -> 0% of each run, Pallas kernels for 0% -> 0%
where the time goes in v1:
time: 55 us; the launch traced here: 54.8 us
  Pallas kernels  46.1 us (84%)
  local copies, waits for them, and re-layouts  4.52 us (8%)
  other arithmetic  4.18 us (8%)
    pallas_call x1, Pallas kernels, local(): pl.pallas_call(functools.partial(clean_kernel, twins, lines), out_shape=j...  46.1 us
    unnamed x8, local copies, waits for them, and re-layouts  4.52 us
    convert_element_type x1, other arithmetic, local(): wide = padded.reshape(channels + 4, rounds, samples).astype(F32)  2.19 us
    add x1, other arithmetic, local(): smooth = 0.5 * middle + 0.25 * (wide[1:channels + 1] + wide[3:channels + 3])  1.99 us

profile of v1, /device:TPU:0, one launch (start us, length us, event | category | flops | bytes accessed | tf_op | source)
XLA Modules:
  0.0 54.8 jit_solution(14073022793169515456)
XLA Ops:
  0.0 0.0 copy-start
  0.0 1.6 %copy-done = bf16[256,8,512]{2,1,0:T(8,128)(2,1)S(1)} copy-done((bf16[256,8,512]{2,1,0:T(8,128)(2,1)S(1)}, bf16[256,8,512]{2,1,0:T(8,128)(2,1)}, u32[]{:S(2)}) %copy-start) | copy-done | bytes 2097176
  1.6 0.0 copy-start.1
  1.6 1.6 %copy-done.1 = bf16[4,512,512]{2,1,0:T(8,128)(2,1)S(1)} copy-done((bf16[4,512,512]{2,1,0:T(8,128)(2,1)S(1)}, bf16[4,512,512]{2,1,0:T(8,128)(2,1)}, u32[]{:S(2)}) %copy-start.1) | copy-done | bytes 2097176
  3.2 0.0 copy-start.2
  3.2 0.7 %copy-done.2 = s32[4,4]{1,0:T(4,128)S(1)} copy-done((s32[4,4]{1,0:T(4,128)S(1)}, s32[4,4]{1,0:T(4,128)}, u32[]{:S(2)}) %copy-start.2) | copy-done | bytes 88
  3.9 0.0 copy-start.3
  3.9 0.7 %copy-done.3 = s32[4]{0:T(128)S(1)} copy-done((s32[4]{0:T(128)S(1)}, s32[4]{0:T(128)}, u32[]{:S(2)}) %copy-start.3) | copy-done | bytes 40
  4.5 46.1 %shard_map.46 = bf16[2080,512]{1,0:T(8,128)(2,1)} custom-call(s32[4]{0:T(128)S(1)} %copy-done.3, s32[4,4]{1,0:T(4,128)S(1)} %copy-done.2, bf16[2048,512]{1,0:T(8,128)(2,1)S(1)} %bitcast.4, bf16[2048,512]{1,0:T(8,128)(2,1)S(1)} %bitcast.5), custom_call_target="tpu_custom_call" | custom-call | flops 7000000000 | bytes 6291456 | tf_op jit(solution)/shard_map/pallas_call | solution.py:218
  50.6 2.2 %convert_element_type.5 = f32[2080,512]{1,0:T(8,128)S(1)} convert(bf16[2080,512]{1,0:T(8,128)(2,1)} %shard_map.46) | non-fusion elementwise | flops 1064960 | bytes 6389760 | tf_op jit(solution)/shard_map/convert_element_type | solution.py:248
  52.8 2.0 %fusion.3 = bf16[256,8,512]{2,1,0:T(8,128)(2,1)} fusion(f32[2080,512]{1,0:T(8,128)S(1)} %convert_element_type.5), kind=kLoop, calls=%fused_computation.5 | loop fusion | flops 5242880 | bytes 14680064 | tf_op jit(solution)/shard_map/add | solution.py:250
Async XLA Ops:
  0.0 1.6 %copy-start = (bf16[256,8,512]{2,1,0:T(8,128)(2,1)S(1)}, bf16[256,8,512]{2,1,0:T(8,128)(2,1)}, u32[]{:S(2)}) copy-start(bf16[256,8,512]{2,1,0:T(8,128)(2,1)} %param.4) | copy-start | bytes 6291460
  1.6 1.6 %copy-start.1 = (bf16[4,512,512]{2,1,0:T(8,128)(2,1)S(1)}, bf16[4,512,512]{2,1,0:T(8,128)(2,1)}, u32[]{:S(2)}) copy-start(bf16[4,512,512]{2,1,0:T(8,128)(2,1)} %param.7) | copy-start | bytes 6291460
  3.2 0.7 %copy-start.2 = (s32[4,4]{1,0:T(4,128)S(1)}, s32[4,4]{1,0:T(4,128)}, u32[]{:S(2)}) copy-start(s32[4,4]{1,0:T(4,128)} %lag_ref.1) | copy-start | bytes 196
  3.9 0.7 %copy-start.3 = (s32[4]{0:T(128)S(1)}, s32[4]{0:T(128)}, u32[]{:S(2)}) copy-start(s32[4]{0:T(128)} %slip_ref.1) | copy-start | bytes 52

commit v2 on v1

--- a/solution.py
+++ b/solution.py
@@ -9,7 +9,8 @@
 
 MESH = pl.DeviceIdType.MESH
 GROUP = 16
-STEPS = 4
+STEPS = 8
+AHEAD = 3
 F32, BF16 = jnp.float32, jnp.bfloat16
 
 
@@ -18,9 +19,10 @@
 
 
 def clean_kernel(
-    twins, lines, slip_ref, lag_ref, rec_ref, ops_hbm, out_ref,
-    guides, lands, picks, spread, ops_ref, edges,
-    ops_sem, land_send, land_recv, send_sem, recv_sem, edge_send, edge_recv,
+    twins, lines, slip_hbm, lag_hbm, rec_hbm, ops_hbm, out_hbm,
+    slip_ref, lag_ref, rec_ref, ops_ref, out_ref,
+    guides, lands, picks, spread, edges,
+    small_sem, rec_sem, out_sem, land_send, land_recv, send_sem, recv_sem, edge_send, edge_recv,
 ):
     me = lax.axis_index("twin")
     line = lax.axis_index("rcv")
@@ -32,7 +34,22 @@
     block = GROUP * rounds
     per = groups // STEPS
 
-    load_ops = pltpu.make_async_copy(ops_hbm, ops_ref, ops_sem)
+    def chunk(step):
+        return lax.rem(step * (STEPS - 1), STEPS)
+
+    size = rows // STEPS
+
+    def load(step):
+        part = pl.ds(pl.multiple_of(chunk(step) * size, size), size)
+        return pltpu.make_async_copy(rec_hbm.at[part], rec_ref.at[part], rec_sem.at[step])
+
+    load_slip = pltpu.make_async_copy(slip_hbm, slip_ref, small_sem.at[0])
+    load_lag = pltpu.make_async_copy(lag_hbm, lag_ref, small_sem.at[1])
+    load_ops = pltpu.make_async_copy(ops_hbm, ops_ref, small_sem.at[2])
+    load_slip.start()
+    load_lag.start()
+    for step in range(STEPS):
+        load(step).start()
     load_ops.start()
 
     others = [lax.rem(me + d, twins) for d in range(1, twins)]
@@ -43,6 +60,9 @@
     for other in (left, right):
         pl.semaphore_signal(barrier, inc=1, device_id={"rcv": other}, device_id_type=MESH)
 
+    load_slip.wait()
+    load_lag.wait()
+
     order_row, rec_lane = iota((8, 128), 0), (iota((8, 128), 1) // GROUP) % recs
     land = jnp.full((8, 128), -1, jnp.int32)
     for r in range(recs):
@@ -58,9 +78,6 @@
     pick = (row % GROUP == col // rounds) & ((col % rounds) * twins + me == slip)
     pick = jnp.where(pick, 1.0, 0.0).astype(BF16)
 
-    def chunk(step):
-        return lax.rem(step * (STEPS - 1), STEPS)
-
     def own(twin):
         return pl.ds(pl.multiple_of(twin * mine, mine), mine)
 
@@ -72,6 +89,8 @@
         )
 
     def extract(step):
+        load(step).wait()
+
         def one(i, _):
             g = chunk(step) * per + i
             rec = rec_ref[pl.ds(pl.multiple_of(g * block, block), block), :]
@@ -111,13 +130,18 @@
     for d in range(twins - 1):
         land_copy(d).start()
 
-    def send_rest(step, _):
+    def send_next(step, _):
         extract(step)
         for copy in first_copies(step):
             copy.start()
         return 0
 
-    lax.fori_loop(1, STEPS, send_rest, 0)
+    def extract_next(step, _):
+        extract(step)
+        return 0
+
+    lax.fori_loop(1, AHEAD, send_next, 0)
+    lax.fori_loop(AHEAD, STEPS, extract_next, 0)
 
     for d in range(twins - 1):
         land_copy(d).wait()
@@ -155,6 +179,11 @@
             out_ref[pl.ds(pl.multiple_of(at + pad, pad), 2 * block), :] = (rec - noise).astype(BF16)
             return 0
         lax.fori_loop(0, per // 2, one, 0)
+        store(step).start()
+
+    def store(step):
+        part = pl.ds(pl.multiple_of(chunk(step) * size + pad, pad), size)
+        return pltpu.make_async_copy(out_ref.at[part], out_hbm.at[part], out_sem.at[step])
 
     def arrive(step):
         if relay:
@@ -176,19 +205,24 @@
             for k, to in enumerate((left, right))
         ]
 
-    def advance(step, _):
-        arrive(step + 1)
-        finish(step)
-        work(step)
+    def advance(step, more, ready):
+        arrive(step)
+        if more:
+            for copy in first_copies(step + AHEAD):
+                copy.start()
+        if ready:
+            finish(step - 1)
+            work(step - 1)
         return 0
 
-    arrive(0)
-    lax.fori_loop(0, 2, advance, 0)
+    advance(0, True, False)
+    lax.fori_loop(1, 3, lambda step, _: advance(step, True, True), 0)
     edges[0] = out_ref[pad : 2 * pad, :]
     edges[1] = out_ref[rows : rows + pad, :]
     for copy in edge_copies():
         copy.start()
-    lax.fori_loop(2, STEPS - 1, advance, 0)
+    lax.fori_loop(3, STEPS - AHEAD, lambda step, _: advance(step, True, True), 0)
+    lax.fori_loop(STEPS - AHEAD, STEPS, lambda step, _: advance(step, False, True), 0)
     finish(STEPS - 1)
     work(STEPS - 1)
 
@@ -198,12 +232,22 @@
     out_ref[0:pad, :] = jnp.where(line > 0, edges[3], zero)
     out_ref[rows + pad : rows + 2 * pad, :] = jnp.where(line < lines - 1, edges[2], zero)
 
+    ends = [
+        pltpu.make_async_copy(out_ref.at[part], out_hbm.at[part], out_sem.at[STEPS + k])
+        for k, part in enumerate((pl.ds(0, pad), pl.ds(rows + pad, pad)))
+    ]
+    for copy in ends:
+        copy.start()
+
     def sent(step, _):
+        store(step).wait()
         for copy in first_copies(step) + (relays(step) if relay else []):
             copy.wait_send()
         return 0
 
     lax.fori_loop(0, STEPS, sent, 0)
+    for copy in ends:
+        copy.wait()
 
 
 def local(record, slip_block, ghost_lag, order_ops):
@@ -213,21 +257,26 @@
     groups, mine = channels // GROUP, recs * GROUP
     block = GROUP * rounds
     ways = max(twins, 4)
-    vmem = pl.BlockSpec(memory_space=pltpu.VMEM)
-    smem = pl.BlockSpec(memory_space=pltpu.SMEM)
+    far = pl.BlockSpec(memory_space=pl.ANY)
     padded = pl.pallas_call(
         functools.partial(clean_kernel, twins, lines),
         out_shape=jax.ShapeDtypeStruct(((channels + 4) * rounds, samples), BF16),
-        in_specs=[smem, smem, vmem, pl.BlockSpec(memory_space=pl.ANY)],
-        out_specs=vmem,
+        in_specs=[far] * 4,
+        out_specs=far,
         scratch_shapes=[
+            pltpu.SMEM((recs,), jnp.int32),
+            pltpu.SMEM((recs, orders), jnp.int32),
+            pltpu.VMEM((channels * rounds, samples), BF16),
+            pltpu.VMEM((orders * samples, samples), BF16),
+            pltpu.VMEM(((channels + 4) * rounds, samples), BF16),
             pltpu.VMEM((groups, twins * mine, samples), BF16),
             pltpu.VMEM((twins, 8, 128), jnp.int32),
             pltpu.VMEM((orders * block, twins * mine), BF16),
             pltpu.VMEM((2 * block, orders * samples), BF16),
-            pltpu.VMEM((orders * samples, samples), BF16),
             pltpu.VMEM((4, 2 * rounds, samples), BF16),
-            pltpu.SemaphoreType.DMA,
+            pltpu.SemaphoreType.DMA((3,)),
+            pltpu.SemaphoreType.DMA((STEPS,)),
+            pltpu.SemaphoreType.DMA((STEPS + 2,)),
             pltpu.SemaphoreType.DMA((twins,)),
             pltpu.SemaphoreType.DMA((twins,)),
             pltpu.SemaphoreType.DMA((STEPS, ways)),
@@ -236,7 +285,7 @@
             pltpu.SemaphoreType.DMA((2,)),
         ],
         compiler_params=pltpu.CompilerParams(
-            collective_id=0, has_side_effects=True, vmem_limit_bytes=48 * 2**20
+            collective_id=0, has_side_effects=True, vmem_limit_bytes=60 * 2**20
         ),
         cost_estimate=pl.CostEstimate(
             flops=7 * 10**9, bytes_accessed=6 * 2**20, transcendentals=0
@@ -245,10 +294,9 @@
         slip_block, ghost_lag, record.reshape(channels * rounds, samples),
         order_ops.reshape(orders * samples, samples),
     )
-    wide = padded.reshape(channels + 4, rounds, samples).astype(F32)
-    middle = wide[2 : channels + 2]
-    smooth = 0.5 * middle + 0.25 * (wide[1 : channels + 1] + wide[3 : channels + 3])
-    return smooth.astype(BF16)
+    wide = padded.reshape(channels + 4, rounds, samples)
+    before, middle, after = (wide[k : channels + k].astype(F32) for k in (1, 2, 3))
+    return (0.5 * middle + 0.25 * (before + after)).astype(BF16)
 
 
 def solution(mesh):

time: 55 us -> 50.3 us (0.915)
  local copies, waits for them, and re-layouts: 4.52 us -> 0 us
  Pallas kernels: 46.1 us -> 44.9 us
  other arithmetic: 4.18 us -> 5.25 us
    unnamed x8 -> x0, local copies, waits for them, and re-layouts: 4.52 us -> none
    add x1, other arithmetic: 1.99 us -> 5.25 us  [local(): return (0.5 * middle + 0.25 * (before + after)).astype(BF16)]
    convert_element_type x1 -> x0, other arithmetic: 2.19 us -> none  [local(): wide = padded.reshape(channels + 4, rounds, samples).astype(F32)]
    pallas_call x1, Pallas kernels: 46.1 us -> 44.9 us  [local(): pl.pallas_call(functools.partial(clean_kernel, twins, lines), out_shape=j...]
where the time goes in v2:
time: 50.3 us; the launch traced here: 50.1 us
  Pallas kernels  44.9 us (89%)
  other arithmetic  5.25 us (10%)
    pallas_call x1, Pallas kernels, local(): pl.pallas_call(functools.partial(clean_kernel, twins, lines), out_shape=j...  44.9 us
    add x1, other arithmetic, local(): return (0.5 * middle + 0.25 * (before + after)).astype(BF16)  5.25 us

profile of v2, /device:TPU:0, one launch (start us, length us, event | category | flops | bytes accessed | tf_op | source)
XLA Modules:
  0.0 50.1 jit_solution(11569678910809819384)
XLA Ops:
  0.0 44.9 %shard_map.46 = bf16[2080,512]{1,0:T(8,128)(2,1)} custom-call(s32[4]{0:T(128)} %slip_hbm.1, s32[4,4]{1,0:T(4,128)} %lag_hbm.1, bf16[2048,512]{1,0:T(8,128)(2,1)} %bitcast.4, bf16[2048,512]{1,0:T(8,128)(2,1)} %bitcast.5), custom_call_target="tpu_custom_call" | custom-call | flops 7000000000 | bytes 6291456 | tf_op jit(solution)/shard_map/pallas_call | solution.py:261
  44.9 5.2 %fusion = bf16[256,8,512]{2,1,0:T(8,128)(2,1)} fusion(bf16[2080,512]{1,0:T(8,128)(2,1)} %shard_map.46), kind=kLoop, calls=%fused_computation.1 | loop fusion | flops 8388608 | bytes 8388608 | tf_op jit(solution)/shard_map/add | solution.py:299

commit v3 on v2

--- a/solution.py
+++ b/solution.py
@@ -20,7 +20,7 @@
 
 def clean_kernel(
     twins, lines, slip_hbm, lag_hbm, rec_hbm, ops_hbm, out_hbm,
-    slip_ref, lag_ref, rec_ref, ops_ref, out_ref,
+    slip_ref, lag_ref, rec_ref, ops_ref, clean, out_ref,
     guides, lands, picks, spread, edges,
     small_sem, rec_sem, out_sem, land_send, land_recv, send_sem, recv_sem, edge_send, edge_recv,
 ):
@@ -176,14 +176,24 @@
             at = (chunk(step) * per + i * 2) * block
             at = pl.multiple_of(at, 2 * block)
             rec = rec_ref[pl.ds(at, 2 * block), :].astype(F32)
-            out_ref[pl.ds(pl.multiple_of(at + pad, pad), 2 * block), :] = (rec - noise).astype(BF16)
+            clean[pl.ds(pl.multiple_of(at + pad, pad), 2 * block), :] = (rec - noise).astype(BF16)
             return 0
         lax.fori_loop(0, per // 2, one, 0)
-        store(step).start()
-
-    def store(step):
-        part = pl.ds(pl.multiple_of(chunk(step) * size + pad, pad), size)
-        return pltpu.make_async_copy(out_ref.at[part], out_hbm.at[part], out_sem.at[step])
+
+    def store(begin, count, index):
+        part = pl.ds(pl.multiple_of(begin * rounds, pad), count * rounds)
+        return pltpu.make_async_copy(out_ref.at[part], out_hbm.at[part], out_sem.at[index])
+
+    def smooth(begin, count, index):
+        at = pl.multiple_of(begin * rounds, pad)
+        wide = clean[pl.ds(at, (count + 4) * rounds), :].astype(F32)
+        before, middle, after = (
+            wide[k * rounds : (k + count) * rounds] for k in (1, 2, 3)
+        )
+        out_ref[pl.ds(at, count * rounds), :] = (
+            0.5 * middle + 0.25 * (before + after)
+        ).astype(BF16)
+        store(begin, count, index).start()
 
     def arrive(step):
         if relay:
@@ -205,7 +215,12 @@
             for k, to in enumerate((left, right))
         ]
 
-    def advance(step, more, ready):
+    chans = per * GROUP
+
+    def window(step):
+        return chunk(step) * chans + 2, chans, step
+
+    def advance(step, more, ready, settled):
         arrive(step)
         if more:
             for copy in first_copies(step + AHEAD):
@@ -213,41 +228,49 @@
         if ready:
             finish(step - 1)
             work(step - 1)
-        return 0
-
-    advance(0, True, False)
-    lax.fori_loop(1, 3, lambda step, _: advance(step, True, True), 0)
-    edges[0] = out_ref[pad : 2 * pad, :]
-    edges[1] = out_ref[rows : rows + pad, :]
+        if settled:
+            smooth(*window(step - 1))
+        return 0
+
+    advance(0, True, False, False)
+    lax.fori_loop(1, 3, lambda step, _: advance(step, True, True, False), 0)
+    edges[0] = clean[pad : 2 * pad, :]
+    edges[1] = clean[rows : rows + pad, :]
     for copy in edge_copies():
         copy.start()
-    lax.fori_loop(3, STEPS - AHEAD, lambda step, _: advance(step, True, True), 0)
-    lax.fori_loop(STEPS - AHEAD, STEPS, lambda step, _: advance(step, False, True), 0)
-    finish(STEPS - 1)
-    work(STEPS - 1)
+    lax.fori_loop(3, STEPS - AHEAD, lambda step, _: advance(step, True, True, True), 0)
+    lax.fori_loop(STEPS - AHEAD, STEPS, lambda step, _: advance(step, False, True, True), 0)
 
     for copy in edge_copies():
         copy.wait()
     zero = jnp.zeros((pad, samples), BF16)
-    out_ref[0:pad, :] = jnp.where(line > 0, edges[3], zero)
-    out_ref[rows + pad : rows + 2 * pad, :] = jnp.where(line < lines - 1, edges[2], zero)
-
-    ends = [
-        pltpu.make_async_copy(out_ref.at[part], out_hbm.at[part], out_sem.at[STEPS + k])
-        for k, part in enumerate((pl.ds(0, pad), pl.ds(rows + pad, pad)))
+    clean[0:pad, :] = jnp.where(line > 0, edges[3], zero)
+    clean[rows + pad : rows + 2 * pad, :] = jnp.where(line < lines - 1, edges[2], zero)
+    last = [
+        (0, chans - 2, 0),
+        ((STEPS - 1) * chans + 2, chans - 2, 1),
+        (chans - 2, chans + 4, STEPS - 1),
     ]
-    for copy in ends:
-        copy.start()
+    smooth(*last[0])
+    smooth(*last[1])
+    finish(STEPS - 1)
+    work(STEPS - 1)
+    smooth(*last[2])
 
     def sent(step, _):
-        store(step).wait()
         for copy in first_copies(step) + (relays(step) if relay else []):
             copy.wait_send()
         return 0
 
     lax.fori_loop(0, STEPS, sent, 0)
-    for copy in ends:
-        copy.wait()
+
+    def stored(step, _):
+        store(*window(step)).wait()
+        return 0
+
+    lax.fori_loop(2, STEPS - 1, stored, 0)
+    for piece in last:
+        store(*piece).wait()
 
 
 def local(record, slip_block, ghost_lag, order_ops):
@@ -258,9 +281,9 @@
     block = GROUP * rounds
     ways = max(twins, 4)
     far = pl.BlockSpec(memory_space=pl.ANY)
-    padded = pl.pallas_call(
+    smoothed = pl.pallas_call(
         functools.partial(clean_kernel, twins, lines),
-        out_shape=jax.ShapeDtypeStruct(((channels + 4) * rounds, samples), BF16),
+        out_shape=jax.ShapeDtypeStruct((channels * rounds, samples), BF16),
         in_specs=[far] * 4,
         out_specs=far,
         scratch_shapes=[
@@ -269,6 +292,7 @@
             pltpu.VMEM((channels * rounds, samples), BF16),
             pltpu.VMEM((orders * samples, samples), BF16),
             pltpu.VMEM(((channels + 4) * rounds, samples), BF16),
+            pltpu.VMEM((channels * rounds, samples), BF16),
             pltpu.VMEM((groups, twins * mine, samples), BF16),
             pltpu.VMEM((twins, 8, 128), jnp.int32),
             pltpu.VMEM((orders * block, twins * mine), BF16),
@@ -276,7 +300,7 @@
             pltpu.VMEM((4, 2 * rounds, samples), BF16),
             pltpu.SemaphoreType.DMA((3,)),
             pltpu.SemaphoreType.DMA((STEPS,)),
-            pltpu.SemaphoreType.DMA((STEPS + 2,)),
+            pltpu.SemaphoreType.DMA((STEPS,)),
             pltpu.SemaphoreType.DMA((twins,)),
             pltpu.SemaphoreType.DMA((twins,)),
             pltpu.SemaphoreType.DMA((STEPS, ways)),
@@ -294,9 +318,7 @@
         slip_block, ghost_lag, record.reshape(channels * rounds, samples),
         order_ops.reshape(orders * samples, samples),
     )
-    wide = padded.reshape(channels + 4, rounds, samples)
-    before, middle, after = (wide[k : channels + k].astype(F32) for k in (1, 2, 3))
-    return (0.5 * middle + 0.25 * (before + after)).astype(BF16)
+    return smoothed.reshape(channels, rounds, samples)
 
 
 def solution(mesh):

time: 50.3 us -> 48.1 us (0.956)
  other arithmetic: 5.25 us -> 0 us
  local copies, waits for them, and re-layouts: 0 us -> 3.05 us
    add x1 -> x0, other arithmetic: 5.25 us -> none  [local(): return (0.5 * middle + 0.25 * (before + after)).astype(BF16)]
    unnamed x0 -> x1, local copies, waits for them, and re-layouts: none -> 3.05 us
where the time goes in v3:
time: 48.1 us; the launch traced here: 48 us
  Pallas kernels  44.9 us (93%)
  local copies, waits for them, and re-layouts  3.05 us (6%)
    pallas_call x1, Pallas kernels, local(): pl.pallas_call(functools.partial(clean_kernel, twins, lines), out_shape=j...  44.9 us
    unnamed x1, local copies, waits for them, and re-layouts  3.05 us

profile of v3, /device:TPU:0, one launch (start us, length us, event | category | flops | bytes accessed | tf_op | source)
XLA Modules:
  0.0 48.0 jit_solution(8554178196766049120)
XLA Ops:
  0.0 44.9 %shard_map.46 = bf16[2048,512]{1,0:T(8,128)(2,1)} custom-call(s32[4]{0:T(128)} %slip_hbm.1, s32[4,4]{1,0:T(4,128)} %lag_hbm.1, bf16[2048,512]{1,0:T(8,128)(2,1)} %bitcast.4, bf16[2048,512]{1,0:T(8,128)(2,1)} %bitcast.5), custom_call_target="tpu_custom_call" | custom-call | flops 7000000000 | bytes 6291456 | tf_op jit(solution)/shard_map/pallas_call | solution.py:284
  44.9 3.0 %copy.6 = bf16[256,8,512]{2,1,0:T(8,128)(2,1)} copy(bf16[256,8,512]{2,1,0:T(8,128)(2,1)} %bitcast.3) | data formatting | bytes 4194304

commit v4 on v3

--- a/solution.py
+++ b/solution.py
@@ -19,10 +19,10 @@
 
 
 def clean_kernel(
-    twins, lines, slip_hbm, lag_hbm, rec_hbm, ops_hbm, out_hbm,
-    slip_ref, lag_ref, rec_ref, ops_ref, clean, out_ref,
+    twins, lines, slip_hbm, lag_hbm, rec_hbm, ops_hbm, out_ref,
+    slip_ref, lag_ref, rec_ref, ops_ref, clean,
     guides, lands, picks, spread, edges,
-    small_sem, rec_sem, out_sem, land_send, land_recv, send_sem, recv_sem, edge_send, edge_recv,
+    small_sem, rec_sem, land_send, land_recv, send_sem, recv_sem, edge_send, edge_recv,
 ):
     me = lax.axis_index("twin")
     line = lax.axis_index("rcv")
@@ -180,11 +180,7 @@
             return 0
         lax.fori_loop(0, per // 2, one, 0)
 
-    def store(begin, count, index):
-        part = pl.ds(pl.multiple_of(begin * rounds, pad), count * rounds)
-        return pltpu.make_async_copy(out_ref.at[part], out_hbm.at[part], out_sem.at[index])
-
-    def smooth(begin, count, index):
+    def smooth(begin, count):
         at = pl.multiple_of(begin * rounds, pad)
         wide = clean[pl.ds(at, (count + 4) * rounds), :].astype(F32)
         before, middle, after = (
@@ -193,7 +189,6 @@
         out_ref[pl.ds(at, count * rounds), :] = (
             0.5 * middle + 0.25 * (before + after)
         ).astype(BF16)
-        store(begin, count, index).start()
 
     def arrive(step):
         if relay:
@@ -218,7 +213,7 @@
     chans = per * GROUP
 
     def window(step):
-        return chunk(step) * chans + 2, chans, step
+        return chunk(step) * chans + 2, chans
 
     def advance(step, more, ready, settled):
         arrive(step)
@@ -246,16 +241,11 @@
     zero = jnp.zeros((pad, samples), BF16)
     clean[0:pad, :] = jnp.where(line > 0, edges[3], zero)
     clean[rows + pad : rows + 2 * pad, :] = jnp.where(line < lines - 1, edges[2], zero)
-    last = [
-        (0, chans - 2, 0),
-        ((STEPS - 1) * chans + 2, chans - 2, 1),
-        (chans - 2, chans + 4, STEPS - 1),
-    ]
-    smooth(*last[0])
-    smooth(*last[1])
+    smooth(0, chans - 2)
+    smooth((STEPS - 1) * chans + 2, chans - 2)
     finish(STEPS - 1)
     work(STEPS - 1)
-    smooth(*last[2])
+    smooth(chans - 2, chans + 4)
 
     def sent(step, _):
         for copy in first_copies(step) + (relays(step) if relay else []):
@@ -263,14 +253,6 @@
         return 0
 
     lax.fori_loop(0, STEPS, sent, 0)
-
-    def stored(step, _):
-        store(*window(step)).wait()
-        return 0
-
-    lax.fori_loop(2, STEPS - 1, stored, 0)
-    for piece in last:
-        store(*piece).wait()
 
 
 def local(record, slip_block, ghost_lag, order_ops):
@@ -280,26 +262,24 @@
     groups, mine = channels // GROUP, recs * GROUP
     block = GROUP * rounds
     ways = max(twins, 4)
-    far = pl.BlockSpec(memory_space=pl.ANY)
+    far = pl.BlockSpec(memory_space=pltpu.HBM)
     smoothed = pl.pallas_call(
         functools.partial(clean_kernel, twins, lines),
-        out_shape=jax.ShapeDtypeStruct((channels * rounds, samples), BF16),
+        out_shape=pltpu.VMEM((channels * rounds, samples), BF16),
         in_specs=[far] * 4,
-        out_specs=far,
+        out_specs=pl.BlockSpec(memory_space=pltpu.VMEM),
         scratch_shapes=[
             pltpu.SMEM((recs,), jnp.int32),
             pltpu.SMEM((recs, orders), jnp.int32),
             pltpu.VMEM((channels * rounds, samples), BF16),
             pltpu.VMEM((orders * samples, samples), BF16),
             pltpu.VMEM(((channels + 4) * rounds, samples), BF16),
-            pltpu.VMEM((channels * rounds, samples), BF16),
             pltpu.VMEM((groups, twins * mine, samples), BF16),
             pltpu.VMEM((twins, 8, 128), jnp.int32),
             pltpu.VMEM((orders * block, twins * mine), BF16),
             pltpu.VMEM((2 * block, orders * samples), BF16),
             pltpu.VMEM((4, 2 * rounds, samples), BF16),
             pltpu.SemaphoreType.DMA((3,)),
-            pltpu.SemaphoreType.DMA((STEPS,)),
             pltpu.SemaphoreType.DMA((STEPS,)),
             pltpu.SemaphoreType.DMA((twins,)),
             pltpu.SemaphoreType.DMA((twins,)),
@@ -309,7 +289,7 @@
             pltpu.SemaphoreType.DMA((2,)),
         ],
         compiler_params=pltpu.CompilerParams(
-            collective_id=0, has_side_effects=True, vmem_limit_bytes=60 * 2**20
+            collective_id=0, has_side_effects=True, vmem_limit_bytes=56 * 2**20
         ),
         cost_estimate=pl.CostEstimate(
             flops=7 * 10**9, bytes_accessed=6 * 2**20, transcendentals=0

time: 48.1 us -> 45.7 us (0.950)
  local copies, waits for them, and re-layouts: 3.05 us -> 1.32 us
  Pallas kernels: 44.9 us -> 44.2 us
    unnamed x1, local copies, waits for them, and re-layouts: 3.05 us -> 1.32 us
    pallas_call x1, Pallas kernels: 44.9 us -> 44.2 us  [local(): pl.pallas_call(functools.partial(clean_kernel, twins, lines), out_shape=p...]
where the time goes in v4:
time: 45.7 us; the launch traced here: 45.5 us
  Pallas kernels  44.2 us (97%)
  local copies, waits for them, and re-layouts  1.32 us (3%)
    pallas_call x1, Pallas kernels, local(): pl.pallas_call(functools.partial(clean_kernel, twins, lines), out_shape=p...  44.2 us
    unnamed x1, local copies, waits for them, and re-layouts  1.32 us

profile of v4, /device:TPU:0, one launch (start us, length us, event | category | flops | bytes accessed | tf_op | source)
XLA Modules:
  0.0 45.5 jit_solution(5849836561681083292)
XLA Ops:
  0.0 44.2 %shard_map.46 = bf16[2048,512]{1,0:T(8,128)(2,1)S(1)} custom-call(s32[4]{0:T(128)} %slip_hbm.1, s32[4,4]{1,0:T(4,128)} %lag_hbm.1, bf16[2048,512]{1,0:T(8,128)(2,1)} %bitcast.4, bf16[2048,512]{1,0:T(8,128)(2,1)} %bitcast.5), custom_call_target="tpu_custom_call" | custom-call | flops 7000000000 | bytes 6291456 | tf_op jit(solution)/shard_map/pallas_call | solution.py:266
  44.2 1.3 %copy.6 = bf16[256,8,512]{2,1,0:T(8,128)(2,1)} copy(bf16[256,8,512]{2,1,0:T(8,128)(2,1)S(1)} %bitcast.3) | data formatting | bytes 4194304

commit v5 on v4

--- a/solution.py
+++ b/solution.py
@@ -9,8 +9,8 @@
 
 MESH = pl.DeviceIdType.MESH
 GROUP = 16
-STEPS = 8
-AHEAD = 3
+STEPS = 16
+AHEAD = 5
 F32, BF16 = jnp.float32, jnp.bfloat16
 
 
@@ -78,11 +78,13 @@
     pick = (row % GROUP == col // rounds) & ((col % rounds) * twins + me == slip)
     pick = jnp.where(pick, 1.0, 0.0).astype(BF16)
 
-    def own(twin):
-        return pl.ds(pl.multiple_of(twin * mine, mine), mine)
+    half = mine // 2
+
+    def own(twin, begin=0, count=mine):
+        return pl.ds(pl.multiple_of(twin * mine + begin, half), count)
 
     def move(step, begin, count, twin, to, index):
-        part = guides.at[pl.ds(chunk(step) * per + begin, count), own(twin)]
+        part = guides.at[pl.ds(chunk(step) * per, per), own(twin, begin, count)]
         return pltpu.make_async_remote_copy(
             src_ref=part, dst_ref=part, send_sem=send_sem.at[step, index],
             recv_sem=recv_sem.at[step, index], device_id={"twin": to}, device_id_type=MESH,
@@ -103,17 +105,16 @@
     if relay:
         across = (me // 2) * 2 + (1 - me % 2)
         along = (1 - me // 2) * 2 + me % 2
-        half = per // 2
 
     def first_copies(step):
         if relay:
-            return [move(step, 0, per, me, across, 0), move(step, 0, per, me, along, 1)]
-        return [move(step, 0, per, me, other, d) for d, other in enumerate(others)]
+            return [move(step, 0, mine, me, across, 0), move(step, 0, mine, me, along, 1)]
+        return [move(step, 0, mine, me, other, d) for d, other in enumerate(others)]
 
     def relays(step):
         return [
             move(step, 0, half, along, across, 2),
-            move(step, half, per - half, across, along, 3),
+            move(step, half, half, across, along, 3),
         ]
 
     extract(0)
@@ -164,21 +165,17 @@
     pad = 2 * rounds
 
     def work(step):
-        def one(i, _):
-            for k in range(2):
-                g = chunk(step) * per + i * 2 + k
-                landed = jnp.dot(picks[...], guides[g], preferred_element_type=F32).astype(BF16)
-                for h in range(orders):
-                    spread[k * block : (k + 1) * block, h * samples : (h + 1) * samples] = landed[
-                        h * block : (h + 1) * block
-                    ]
-            noise = jnp.dot(spread[...], ops_ref[...], preferred_element_type=F32)
-            at = (chunk(step) * per + i * 2) * block
-            at = pl.multiple_of(at, 2 * block)
-            rec = rec_ref[pl.ds(at, 2 * block), :].astype(F32)
-            clean[pl.ds(pl.multiple_of(at + pad, pad), 2 * block), :] = (rec - noise).astype(BF16)
-            return 0
-        lax.fori_loop(0, per // 2, one, 0)
+        for k in range(per):
+            g = chunk(step) * per + k
+            landed = jnp.dot(picks[...], guides[g], preferred_element_type=F32).astype(BF16)
+            for h in range(orders):
+                spread[k * block : (k + 1) * block, h * samples : (h + 1) * samples] = landed[
+                    h * block : (h + 1) * block
+                ]
+        noise = jnp.dot(spread[...], ops_ref[...], preferred_element_type=F32)
+        at = pl.multiple_of(chunk(step) * size, size)
+        rec = rec_ref[pl.ds(at, size), :].astype(F32)
+        clean[pl.ds(pl.multiple_of(at + pad, pad), size), :] = (rec - noise).astype(BF16)
 
     def smooth(begin, count):
         at = pl.multiple_of(begin * rounds, pad)
@@ -277,7 +274,7 @@
             pltpu.VMEM((groups, twins * mine, samples), BF16),
             pltpu.VMEM((twins, 8, 128), jnp.int32),
             pltpu.VMEM((orders * block, twins * mine), BF16),
-            pltpu.VMEM((2 * block, orders * samples), BF16),
+            pltpu.VMEM((channels * rounds // STEPS, orders * samples), BF16),
             pltpu.VMEM((4, 2 * rounds, samples), BF16),
             pltpu.SemaphoreType.DMA((3,)),
             pltpu.SemaphoreType.DMA((STEPS,)),

time: 45.7 us -> 49.5 us (1.083)
  Pallas kernels: 44.2 us -> 48 us
    pallas_call x1, Pallas kernels: 44.2 us -> 48 us  [local(): pl.pallas_call(functools.partial(clean_kernel, twins, lines), out_shape=p...]
where the time goes in v5:
time: 49.5 us; the launch traced here: 49.4 us
  Pallas kernels  48 us (97%)
  local copies, waits for them, and re-layouts  1.32 us (3%)
    pallas_call x1, Pallas kernels, local(): pl.pallas_call(functools.partial(clean_kernel, twins, lines), out_shape=p...  48 us
    unnamed x1, local copies, waits for them, and re-layouts  1.32 us

profile of v5, /device:TPU:0, one launch (start us, length us, event | category | flops | bytes accessed | tf_op | source)
XLA Modules:
  0.0 49.4 jit_solution(2473718870468008323)
XLA Ops:
  0.0 48.0 %shard_map.46 = bf16[2048,512]{1,0:T(8,128)(2,1)S(1)} custom-call(s32[4]{0:T(128)} %slip_hbm.1, s32[4,4]{1,0:T(4,128)} %lag_hbm.1, bf16[2048,512]{1,0:T(8,128)(2,1)} %bitcast.4, bf16[2048,512]{1,0:T(8,128)(2,1)} %bitcast.5), custom_call_target="tpu_custom_call" | custom-call | flops 7000000000 | bytes 6291456 | tf_op jit(solution)/shard_map/pallas_call | solution.py:263
  48.0 1.3 %copy.6 = bf16[256,8,512]{2,1,0:T(8,128)(2,1)} copy(bf16[256,8,512]{2,1,0:T(8,128)(2,1)S(1)} %bitcast.3) | data formatting | bytes 4194304

commit v6 on v4

--- a/solution.py
+++ b/solution.py
@@ -10,7 +10,7 @@
 MESH = pl.DeviceIdType.MESH
 GROUP = 16
 STEPS = 8
-AHEAD = 3
+AHEAD = 2
 F32, BF16 = jnp.float32, jnp.bfloat16
 
 

time: 45.7 us -> 45.1 us (0.987)
  Pallas kernels: 44.2 us -> 43.6 us
    pallas_call x1, Pallas kernels: 44.2 us -> 43.6 us  [local(): pl.pallas_call(functools.partial(clean_kernel, twins, lines), out_shape=p...]
where the time goes in v6:
time: 45.1 us; the launch traced here: 45 us
  Pallas kernels  43.6 us (97%)
  local copies, waits for them, and re-layouts  1.32 us (3%)
    pallas_call x1, Pallas kernels, local(): pl.pallas_call(functools.partial(clean_kernel, twins, lines), out_shape=p...  43.6 us
    unnamed x1, local copies, waits for them, and re-layouts  1.32 us

profile of v6, /device:TPU:0, one launch (start us, length us, event | category | flops | bytes accessed | tf_op | source)
XLA Modules:
  0.0 45.0 jit_solution(12702489486506470436)
XLA Ops:
  0.0 43.6 %shard_map.46 = bf16[2048,512]{1,0:T(8,128)(2,1)S(1)} custom-call(s32[4]{0:T(128)} %slip_hbm.1, s32[4,4]{1,0:T(4,128)} %lag_hbm.1, bf16[2048,512]{1,0:T(8,128)(2,1)} %bitcast.4, bf16[2048,512]{1,0:T(8,128)(2,1)} %bitcast.5), custom_call_target="tpu_custom_call" | custom-call | flops 7000000000 | bytes 6291456 | tf_op jit(solution)/shard_map/pallas_call | solution.py:266
  43.7 1.3 %copy.6 = bf16[256,8,512]{2,1,0:T(8,128)(2,1)} copy(bf16[256,8,512]{2,1,0:T(8,128)(2,1)S(1)} %bitcast.3) | data formatting | bytes 4194304

commit v7 on v6

--- a/solution.py
+++ b/solution.py
@@ -10,7 +10,7 @@
 MESH = pl.DeviceIdType.MESH
 GROUP = 16
 STEPS = 8
-AHEAD = 2
+AHEAD = 1
 F32, BF16 = jnp.float32, jnp.bfloat16
 
 

time: 45.1 us -> 55.1 us (1.22)
  Pallas kernels: 43.6 us -> 53.6 us
    pallas_call x1, Pallas kernels: 43.6 us -> 53.6 us  [local(): pl.pallas_call(functools.partial(clean_kernel, twins, lines), out_shape=p...]
where the time goes in v7:
time: 55.1 us; the launch traced here: 54.9 us
  Pallas kernels  53.6 us (97%)
  local copies, waits for them, and re-layouts  1.32 us (2%)
    pallas_call x1, Pallas kernels, local(): pl.pallas_call(functools.partial(clean_kernel, twins, lines), out_shape=p...  53.6 us
    unnamed x1, local copies, waits for them, and re-layouts  1.32 us

profile of v7, /device:TPU:0, one launch (start us, length us, event | category | flops | bytes accessed | tf_op | source)
XLA Modules:
  0.0 54.9 jit_solution(7067207794307814586)
XLA Ops:
  0.0 53.6 %shard_map.46 = bf16[2048,512]{1,0:T(8,128)(2,1)S(1)} custom-call(s32[4]{0:T(128)} %slip_hbm.1, s32[4,4]{1,0:T(4,128)} %lag_hbm.1, bf16[2048,512]{1,0:T(8,128)(2,1)} %bitcast.4, bf16[2048,512]{1,0:T(8,128)(2,1)} %bitcast.5), custom_call_target="tpu_custom_call" | custom-call | flops 7000000000 | bytes 6291456 | tf_op jit(solution)/shard_map/pallas_call | solution.py:266
  53.6 1.3 %copy.6 = bf16[256,8,512]{2,1,0:T(8,128)(2,1)} copy(bf16[256,8,512]{2,1,0:T(8,128)(2,1)S(1)} %bitcast.3) | data formatting | bytes 4194304
